TPU v7x, 256 devices: a whole 4x4x8 slice. The times are simulated.
256 devices in a mesh: resp: 64 (over y_hi, x, z), head: 4 (over y_lo, core).
Axes of the slice: x: 4, y: 4 (y_hi: 2, y_lo: 2; y = y_hi * 2 + y_lo), z: 8, core: 2. Of those that a mesh axis runs over, the one named last changes fastest.
Arguments:
- queries: bfloat16 [16384, 8192], P('resp', 'head'), may hold values from -240 to 240
- d_out: bfloat16 [16384, 8192], P('resp', 'head'), may hold values from -24 to 24
- prefix_keys: bfloat16 [1024, 1024], P('resp', 'head'), may hold values from -17 to 17
- prefix_values: bfloat16 [1024, 1024], P('resp', 'head'), may hold values from -6 to 6
- k_weight: bfloat16 [8192, 1024], P(None, 'head'), may hold values from -0.0625 to 0.0625
- v_weight: bfloat16 [8192, 1024], P(None, 'head'), may hold values from -0.0625 to 0.0625
- lengths: int32 [64], P('resp'), may hold values from 1 to 256, as said below
Outputs:
- prefix_dk: bfloat16 [1024, 1024], P('resp', 'head')
- prefix_dv: bfloat16 [1024, 1024], P('resp', 'head')
- input_grad: bfloat16 [1024, 8192], P('resp', 'head')
Inputs may be any that keep to these rules, and one draw needn't show every extreme that they name: `lengths`: every response has at least one live token and one response has exactly 256.
All inputs are finite; a program needn't handle non-finite values.
Results may differ from a plain program's by a relative error of at most 0.015.
Values may be sent and summed in bfloat16 or wider, within the bound.
A program may use at most 128 MiB of HBM per device.

v0:
```python
import jax
import jax.numpy as jnp
from jax import lax
from jax.sharding import PartitionSpec as P

HD = 128
LEN = 256


def body(queries, d_out, prefix_keys, prefix_values, k_weight, v_weight, lengths):
    scale = HD ** (-0.5)
    rows = queries.shape[0]
    kv_local = prefix_keys.shape[1] // HD
    group = queries.shape[1] // HD // kv_local
    count_resp = lengths.shape[0]
    position = jnp.arange(rows, dtype=jnp.int32) % LEN
    owner = jnp.arange(rows, dtype=jnp.int32) // LEN
    live = jnp.any(
        (owner[:, None] == jnp.arange(count_resp, dtype=jnp.int32)[None, :])
        & (position[:, None] < lengths[None, :]),
        axis=1,
    )
    masked = jnp.where(live[:, None], d_out, jnp.zeros_like(d_out))
    query_heads = queries.reshape(rows, kv_local, group, HD)
    grad_heads = masked.reshape(rows, kv_local, group, HD)
    key_all, value_all = (
        lax.all_gather(prefix_keys, "resp", axis=0, tiled=True),
        lax.all_gather(prefix_values, "resp", axis=0, tiled=True),
    )
    keys = key_all.reshape(-1, kv_local, HD)
    values = value_all.reshape(-1, kv_local, HD)
    scores = (
        jnp.einsum("tkgd,skd->tkgs", query_heads, keys, preferred_element_type=jnp.float32) * scale
    )
    dprobs = jnp.einsum("tkgd,skd->tkgs", grad_heads, values, preferred_element_type=jnp.float32)
    top = jnp.full((rows, kv_local, group), -jnp.inf, jnp.float32)
    total = jnp.zeros((rows, kv_local, group), jnp.float32)
    weighted = jnp.zeros((rows, kv_local, group), jnp.float32)
    new_top = jnp.max(scores, axis=-1)
    factor = jnp.exp(top - new_top)
    expo = jnp.exp(scores - new_top[..., None])
    top, total, weighted = (
        new_top,
        total * factor + jnp.sum(expo, axis=-1),
        weighted * factor + jnp.sum(expo * dprobs, axis=-1),
    )
    lse = top + jnp.log(total)
    delta = weighted / total
    count = key_all.shape[0]
    keys = key_all.reshape(count, kv_local, HD)
    values = value_all.reshape(count, kv_local, HD)
    scores = (
        jnp.einsum("tkgd,skd->tkgs", query_heads, keys, preferred_element_type=jnp.float32) * scale
    )
    probs = jnp.exp(scores - lse[..., None])
    probs_low = probs.astype(jnp.bfloat16)
    grad_v = jnp.einsum("tkgs,tkgd->skd", probs_low, grad_heads, preferred_element_type=jnp.float32)
    dprobs = jnp.einsum("tkgd,skd->tkgs", grad_heads, values, preferred_element_type=jnp.float32)
    dscores = (probs * (dprobs - delta[..., None]) * scale).astype(jnp.bfloat16)
    grad_k = jnp.einsum("tkgs,tkgd->skd", dscores, query_heads, preferred_element_type=jnp.float32)
    shares = lax.psum_scatter(
        jnp.concatenate(
            [grad_k.reshape(count, kv_local * HD), grad_v.reshape(count, kv_local * HD)], axis=1
        ),
        "resp",
        scatter_dimension=0,
        tiled=True,
    )
    width = kv_local * HD
    dk_low = shares[:, :width].astype(jnp.bfloat16)
    dv_low = shares[:, width:].astype(jnp.bfloat16)
    partial_input = jnp.einsum("pc,dc->pd", dk_low, k_weight, preferred_element_type=jnp.float32)
    partial_input = partial_input + jnp.einsum(
        "pc,dc->pd", dv_low, v_weight, preferred_element_type=jnp.float32
    )
    input_grad = lax.psum_scatter(
        partial_input.astype(jnp.bfloat16), "head", scatter_dimension=1, tiled=True
    )
    return (dk_low, dv_low, input_grad)


def solution(mesh):
    placed = (
        P("resp", "head"),
        P("resp", "head"),
        P("resp", "head"),
        P("resp", "head"),
        P(None, "head"),
        P(None, "head"),
        P("resp"),
    )
    return jax.shard_map(
        body,
        mesh=mesh,
        in_specs=placed,
        out_specs=(P("resp", "head"), P("resp", "head"), P("resp", "head")),
        check_vma=False,
    )
```

profile of v0, /device:TPU:1, one launch (start us, length us, event | category | flops | bytes accessed | tf_op | source)
XLA Modules:
  0.0 820.6 jit_solution(3405192840555796282)
XLA Ops:
  7.2 0.0 reduce-scatter.3.cloned.1.call-start
  7.9 160.7 %all_gather.6 = bf16[1024,256]{1,0:T(8,128)(2,1)S(1)} all-gather(bf16[16,256]{1,0:T(8,128)(2,1)} %param.9), channel_id=1, replica_groups=mesh['resp'=64,'head'=4] {'resp'}, dimensions={0}, use_global_device_ids=true | all-gather | bytes 532480 | tf_op jit(solution)/shard_map/all_gather | solution.py:27
  168.5 1.0 copy.32
  169.5 150.0 %all_gather.7 = bf16[1024,256]{1,0:T(8,128)(2,1)S(1)} all-gather(bf16[16,256]{1,0:T(8,128)(2,1)} %param.10), channel_id=1, replica_groups=mesh['resp'=64,'head'=4] {'resp'}, dimensions={0}, use_global_device_ids=true | all-gather | bytes 532480 | tf_op jit(solution)/shard_map/all_gather | solution.py:28
  319.6 0.2 copy.35
  319.8 1.4 select_bitcast_fusion
  321.2 0.2 copy.54
  321.4 1.5 copy.53
  322.9 3.4 bitcast_reduce_fusion
  326.3 10.4 %fusion = (f32[256,2,8]{0,2,1:T(8,128)}, f32[256,2,8]{0,2,1:T(8,128)}, f32[2,256,8,1024]{1,3,2,0:T(8,128)}) fusion(f32[2,1024,256,8]{2,1,3,0:T(8,128)S(1)} %get-tuple-element.10, f32[256,2,8]{0,2,1:T(8,128)S(1)} %get-tuple-element.9, bf16[1024,2,128,1]{0,2,3,1:T(8,128)(2,1)S(1)} %bitcast.73, bf16[256,2,8,128]{3,2,1,0:T(8,128)(2,1)S(1)} %bitcast.69), kind=kOutput, calls=%fused_computation.2 | convolution fusion | flops 1094705152 | bytes 35176448 | tf_op jit(solution)/shard_map/tkgd,skd->tkgs/dot_general | solution.py:58
  336.7 0.8 add_divide_fusion
  337.6 4.9 fusion.6
  342.4 12.4 %copy.41 = bf16[256,2,8,1024]{3,2,1,0:T(8,128)(2,1)} copy(bf16[256,2,8,1024]{0,3,2,1:T(8,128)(2,1)} %fusion.6) | data formatting | bytes 16777216 | tf_op jit(solution)/shard_map/convert_element_type | solution.py:56
  354.8 5.8 fusion.18
  360.6 2.5 copy.43
  363.1 13.1 %fusion.9 = f32[2,1024,128,1]{1,2,3,0:T(8,128)S(1)} fusion(bf16[256,2,8,128]{0,3,2,1:T(8,128)(2,1)S(1)} %bitcast.68, f32[2,256,8,1024]{1,3,2,0:T(8,128)} %get-tuple-element.11, f32[2,1024,256,8]{2,1,3,0:T(8,128)} %copy-done, f32[256,2,8]{0,2,1:T(8,128)S(1)} %get-tuple-element.5, f32[256,2,8]{0,2,1:T(8,128)S(1)} %get-tuple-element.6), kind=kOutput, calls=%fused_computation.15 | convolution fusion | flops 1098907648 | bytes 35684352 | tf_op jit(solution)/shard_map/tkgs,tkgd->skd/dot_general | solution.py:60
  376.2 0.3 copy.42
  376.5 2.8 pad_maximum_fusion
  379.4 0.0 reduce-scatter.5.cloned.1.call-start
  379.4 362.8 %reduce-scatter.3.cloned.1.call-done = f32[16,512]{1,0:T(8,128)} async-done(((f32[1024,512]{1,0:T(8,128)}), f32[16,512]{1,0:T(8,128)}) %reduce-scatter.3.cloned.1.call-update) | async-done | bytes 32784 | tf_op jit(solution)/shard_map/reduce_scatter | solution.py:61
  742.2 0.8 convert.4
  743.0 3.4 fusion.19
  746.4 4.1 fusion.8
  750.5 63.3 %reduce-scatter.5.cloned.1.call-done = bf16[16,2048]{1,0:T(8,128)(2,1)} async-done(((bf16[16,8192]{1,0:T(8,128)(2,1)}), bf16[16,2048]{1,0:T(8,128)(2,1)}) %reduce-scatter.5.cloned.1.call-update) | async-done | bytes 65552 | tf_op jit(solution)/shard_map/reduce_scatter | solution.py:76
  (10 shorter events, 0.1 us)
Async XLA Ops:
  7.2 735.0 %reduce-scatter.3.cloned.1.call-start = ((), (), s32[]{:S(2)}) async-start(), calls=%async_computation.2 | async-start | bytes 2129920 | tf_op jit(solution)/shard_map/reduce_scatter | solution.py:61
  326.3 11.2 %copy-start = (f32[2,1024,256,8]{2,1,3,0:T(8,128)}, f32[2,1024,256,8]{2,1,3,0:T(8,128)S(1)}, u32[]{:S(2)}) copy-start(f32[2,1024,256,8]{2,1,3,0:T(8,128)S(1)} %get-tuple-element.10) | copy-start | bytes 50331652
  379.4 434.4 %reduce-scatter.5.cloned.1.call-start = ((), (), s32[]{:S(2)}) async-start(), calls=%async_computation.3 | async-start | bytes 327680 | tf_op jit(solution)/shard_map/reduce_scatter | solution.py:76
  743.0 70.8 %copy-start.1 = (bf16[16,256]{1,0:T(8,128)(2,1)}, bf16[16,256]{1,0:T(8,128)(2,1)S(1)}, u32[]{:S(2)}) copy-start(bf16[16,256]{1,0:T(8,128)(2,1)S(1)} %get-tuple-element.7) | copy-start | bytes 24580
  743.0 70.8 %copy-start.2 = (bf16[16,256]{1,0:T(8,128)(2,1)}, bf16[16,256]{1,0:T(8,128)(2,1)S(1)}, u32[]{:S(2)}) copy-start(bf16[16,256]{1,0:T(8,128)(2,1)S(1)} %get-tuple-element.8) | copy-start | bytes 24580
Sparse Core Ops, SparseCore 0:
  379.5 362.6 reduce-scatter.2
  750.6 63.1 reduce-scatter.4
where the time goes:
time: 821 us
  waiting for transfers between devices  426 us (52%)
  blocking collectives  311 us (38%)
  matrix products  40.1 us (5%)
  local copies, waits for them, and re-layouts  18.2 us (2%)
  between operations  14.8 us (2%)
  other arithmetic  10.7 us (1%)
    reduce_scatter x1, waiting for transfers between devices, body(): lax.psum_scatter(jnp.concatenate([grad_k.reshape(count, kv_local * HD), g...  363 us
    all_gather x1, blocking collectives, body(): lax.all_gather(prefix_keys, 'resp', axis=0, tiled=True)  161 us
    all_gather x1, blocking collectives, body(): lax.all_gather(prefix_values, 'resp', axis=0, tiled=True)  150 us
    reduce_scatter x1, waiting for transfers between devices, body(): lax.psum_scatter(partial_input.astype(jnp.bfloat16), 'head', scatter_dime...  63.3 us
  transfers between devices with their start and end apart: 2, of which 2 were waited for; matrix products, arithmetic and copies ran while one was open for 0% of the time, Pallas kernels for 0%

commit v1 on v0

v1 whole, which is shorter than its diff:
```python
import functools
import math

import jax
import jax.numpy as jnp
from jax import lax
from jax.experimental import pallas as pl
from jax.experimental.pallas import tpu as pltpu
from jax.sharding import PartitionSpec as P

HD = 128
NY, NX, NZ = 2, 4, 8
NC = 2
N = 8
MESH = pl.DeviceIdType.MESH
SCALE = HD ** (-0.5)
LOG2E = math.log2(math.e)
F32 = jnp.float32
BF16 = jnp.bfloat16


def place():
    r = lax.axis_index("resp")
    return r // (NX * NZ), (r // NZ) % NX, r % NZ, lax.axis_index("head")


def xy_peer(i):
    y, x, z, h = place()
    return ((y + i // NX) % NY * (NX * NZ) + (x + i % NX) % NX * NZ + z, h)


def xy_back(i):
    return i // NX * NX + (-i) % NX


def z_peer(i):
    y, x, z, h = place()
    return (y * (NX * NZ) + x * NZ + (z + i) % NZ, h)


def z_back(i):
    return (-i) % NZ


XY = (xy_peer, xy_back)
Z = (z_peer, z_back)


def head_peer(i):
    y, x, z, h = place()
    return (lax.axis_index("resp"), (h // NC + i // NC) % 2 * NC + (h + i) % NC)


def nt(a, b):
    return lax.dot_general(a, b, (((1,), (1,)), ((), ())), preferred_element_type=F32)


def send(src, dst, ss, rs, to):
    copy = pltpu.make_async_remote_copy(
        src_ref=src, dst_ref=dst, send_sem=ss, recv_sem=rs, device_id=to, device_id_type=MESH
    )
    copy.start()
    return copy


def kernel(
    q_hbm, g_hbm, k_hbm, v_hbm, kw_hbm, vw_hbm, len_ref,
    dk_ref, dv_ref, in_ref,
    qs, gs, kw, vw, full, outbox, inbox, partial, inbox2, low,
    e_s, dp_s, m_s, l_s, w_s, p_s, ds_s, hsend, hrecv, hown,
    load_sem, own_sem, w_sem, ss, rs, hss, hrs,
):
    heads = qs.shape[0]
    group = heads // 2
    rows = qs.shape[1]

    barrier = pltpu.get_barrier_semaphore()
    for peer, _ in (XY, Z):
        for i in range(1, N):
            pl.semaphore_signal(barrier, inc=1, device_id=peer(i), device_id_type=MESH)
    for i in range(1, 4):
        pl.semaphore_signal(barrier, inc=1, device_id=head_peer(i), device_id_type=MESH)

    own = []
    for j in range(2):
        cols = pl.ds(j * HD, HD)
        own.append(pltpu.make_async_copy(k_hbm.at[:, cols], full.at[j, 0, 0, :, pl.ds(0, HD)], own_sem.at[2 * j]))
        own.append(pltpu.make_async_copy(v_hbm.at[:, cols], full.at[j, 0, 0, :, pl.ds(HD, HD)], own_sem.at[2 * j + 1]))
    for copy in own:
        copy.start()
    loads = []
    for h in range(heads):
        cols = pl.ds(h * HD, HD)
        loads.append(pltpu.make_async_copy(q_hbm.at[:, cols], qs.at[h], load_sem.at[0, h]))
        loads.append(pltpu.make_async_copy(g_hbm.at[:, cols], gs.at[h], load_sem.at[1, h]))
    for copy in loads:
        copy.start()
    weights = [
        pltpu.make_async_copy(kw_hbm, kw, w_sem.at[0]),
        pltpu.make_async_copy(vw_hbm, vw, w_sem.at[1]),
    ]
    for copy in weights:
        copy.start()
    for copy in own:
        copy.wait()
    pl.semaphore_wait(barrier, 2 * (N - 1) + 3)

    first = (XY, Z)
    second = (Z, XY)
    sent = []

    def fan(step, j, axes, src_of, dst_of):
        peer, back = axes
        copies = []
        for i in range(1, N):
            copies.append(
                send(src_of(i), dst_of(back(i)), ss.at[step, j, i], rs.at[step, j, back(i)], peer(i))
            )
        sent.extend(copies)
        return copies

    gather1 = [
        fan(0, j, first[j], lambda i, j=j: full.at[j, 0, 0], lambda b, j=j: full.at[j, 0, b]) for j in range(2)
    ]
    gather2 = []
    for j in range(2):
        for copy in gather1[j]:
            copy.wait_recv()
        gather2.append(
            fan(1, j, second[j], lambda i, j=j: full.at[j, 0], lambda b, j=j: full.at[j, b])
        )

    for copy in loads:
        copy.wait()
    live = lax.broadcasted_iota(jnp.int32, (rows, HD), 0) < len_ref[0]

    def mask(h, carry):
        grad = gs[h]
        gs[h] = jnp.where(live, grad.astype(F32), 0.0).astype(BF16)
        return carry

    lax.fori_loop(0, heads, mask, 0)

    def attend(j):
        def one(h, carry):
            q = qs[j * group + h]
            g = gs[j * group + h]
            for c in range(N):
                kv = full[j, c].reshape(N * 16, 2 * HD)
                s = nt(kv[:, :HD], q) * (SCALE * LOG2E)
                dp = nt(kv[:, HD:], g)
                m = jnp.max(s, axis=0, keepdims=True)
                e = jnp.exp2(s - m)
                m_s[c] = m
                l_s[c] = jnp.sum(e, axis=0, keepdims=True)
                w_s[c] = jnp.sum(e * dp, axis=0, keepdims=True)
                e_s[c] = e
                dp_s[c] = dp
            m = m_s[...]
            f = jnp.exp2(m - jnp.max(m, axis=0, keepdims=True))
            total = jnp.sum(f * l_s[...], axis=0)
            delta = jnp.sum(f * w_s[...], axis=0) / total
            m_s[...] = f / total[None]
            for c in range(N):
                p = e_s[c] * m_s[c]
                p_s[h, c] = p.astype(BF16)
                ds_s[h, c] = (p * (dp_s[c] - delta)).astype(BF16)
            return carry

        lax.fori_loop(0, group, one, 0)

        def products(c, carry):
            dv = jnp.zeros((N * 16, HD), F32)
            dk = jnp.zeros((N * 16, HD), F32)
            for h in range(group):
                dv += jnp.dot(p_s[h, c], gs[j * group + h], preferred_element_type=F32)
                dk += jnp.dot(ds_s[h, c], qs[j * group + h], preferred_element_type=F32)
            outbox[j, c, :, :, :HD] = (dk * SCALE).astype(BF16).reshape(N, 16, HD)
            outbox[j, c, :, :, HD:] = dv.astype(BF16).reshape(N, 16, HD)
            return carry

        lax.fori_loop(0, N, products, 0)
        return fan(2, j, second[j], lambda i: outbox.at[j, i], lambda b: inbox.at[j, b])

    def reduce1(j, copies):
        for copy in copies:
            copy.wait_recv()
        total = outbox[j, 0].astype(F32)
        for i in range(1, N):
            total += inbox[j, i].astype(F32)
        partial[j] = total.astype(BF16)
        return fan(3, j, first[j], lambda i: partial.at[j, i], lambda b: inbox2.at[j, b])

    def reduce2(j, copies):
        for copy in copies:
            copy.wait_recv()
        total = partial[j, 0].astype(F32)
        for i in range(1, N):
            total += inbox2[j, i].astype(F32)
        total = total.astype(BF16)
        cols = slice(j * HD, (j + 1) * HD)
        low[0, :, cols] = total[:, :HD]
        low[1, :, cols] = total[:, HD:]
        dk_ref[:, cols] = total[:, :HD]
        dv_ref[:, cols] = total[:, HD:]

    for copy in gather2[1]:
        copy.wait_recv()
    scatter_b = attend(1)
    for copy in gather2[0]:
        copy.wait_recv()
    scatter_b = reduce1(1, scatter_b)
    scatter_a = attend(0)
    reduce2(1, scatter_b)
    scatter_a = reduce1(0, scatter_a)
    for copy in weights:
        copy.wait()
    reduce2(0, scatter_a)

    width = hown.shape[1]
    step = 512
    me = lax.axis_index("head")
    low_k = low[0]
    low_v = low[1]
    exchange = []
    for i in (2, 3, 1, 0):
        _, dest = head_peer(i)
        for t in range(width // step):
            span = pl.ds(pl.multiple_of(dest * width + t * step, step), step)
            part = nt(low_k, kw[span, :]) + nt(low_v, vw[span, :])
            if i:
                hsend[i - 1, :, t * step:(t + 1) * step] = part.astype(BF16)
            else:
                hown[:, t * step:(t + 1) * step] = part
        if i:
            exchange.append(
                send(hsend.at[i - 1], hrecv.at[i - 1], hss.at[i - 1], hrs.at[i - 1], head_peer(i))
            )
    total = hown[...]
    for copy in exchange:
        copy.wait_recv()
    for i in range(3):
        total += hrecv[i].astype(F32)
    in_ref[...] = total.astype(BF16)
    for copy in sent + exchange:
        copy.wait_send()


def body(queries, d_out, prefix_keys, prefix_values, k_weight, v_weight, lengths):
    rows, width = queries.shape
    heads = width // HD
    d = k_weight.shape[0]
    any_spec = pl.BlockSpec(memory_space=pl.ANY)
    vmem = pl.BlockSpec(memory_space=pltpu.VMEM)
    shard = jax.ShapeDtypeStruct(prefix_keys.shape, BF16)
    return pl.pallas_call(
        kernel,
        name="prefix_gradients",
        out_shape=(shard, shard, jax.ShapeDtypeStruct((16, d // 4), BF16)),
        in_specs=[any_spec] * 6 + [pl.BlockSpec(memory_space=pltpu.SMEM)],
        out_specs=(vmem, vmem, vmem),
        scratch_shapes=[
            pltpu.VMEM((heads, rows, HD), BF16),
            pltpu.VMEM((heads, rows, HD), BF16),
            pltpu.VMEM(k_weight.shape, BF16),
            pltpu.VMEM(v_weight.shape, BF16),
            pltpu.VMEM((2, N, N, 16, 2 * HD), BF16),
            pltpu.VMEM((2, N, N, 16, 2 * HD), BF16),
            pltpu.VMEM((2, N, N, 16, 2 * HD), BF16),
            pltpu.VMEM((2, N, 16, 2 * HD), BF16),
            pltpu.VMEM((2, N, 16, 2 * HD), BF16),
            pltpu.VMEM((2, 16, 2 * HD), BF16),
            pltpu.VMEM((N, N * 16, rows), F32),
            pltpu.VMEM((N, N * 16, rows), F32),
            pltpu.VMEM((N, 1, rows), F32),
            pltpu.VMEM((N, 1, rows), F32),
            pltpu.VMEM((N, 1, rows), F32),
            pltpu.VMEM((heads // 2, N, N * 16, rows), BF16),
            pltpu.VMEM((heads // 2, N, N * 16, rows), BF16),
            pltpu.VMEM((3, 16, d // 4), BF16),
            pltpu.VMEM((3, 16, d // 4), BF16),
            pltpu.VMEM((16, d // 4), F32),
            pltpu.SemaphoreType.DMA((2, heads)),
            pltpu.SemaphoreType.DMA((4,)),
            pltpu.SemaphoreType.DMA((2,)),
            pltpu.SemaphoreType.DMA((4, 2, N)),
            pltpu.SemaphoreType.DMA((4, 2, N)),
            pltpu.SemaphoreType.DMA((3,)),
            pltpu.SemaphoreType.DMA((3,)),
        ],
        compiler_params=pltpu.CompilerParams(
            collective_id=0, has_side_effects=True, vmem_limit_bytes=48 * 1024 * 1024
        ),
    )(queries, d_out, prefix_keys, prefix_values, k_weight, v_weight, lengths)


def solution(mesh):
    placed = (
        P("resp", "head"),
        P("resp", "head"),
        P("resp", "head"),
        P("resp", "head"),
        P(None, "head"),
        P(None, "head"),
        P("resp"),
    )
    return jax.shard_map(
        body,
        mesh=mesh,
        in_specs=placed,
        out_specs=(P("resp", "head"), P("resp", "head"), P("resp", "head")),
        check_vma=False,
    )
```

time: 821 us -> 80.3 us (0.10)
  waiting for transfers between devices: 426 us -> 0 us
  blocking collectives: 311 us -> 0 us
  Pallas kernels: 0 us -> 73.1 us
  matrix products: 40.1 us -> 0 us
  between operations: 14.8 us -> 1.3 us
  local copies, waits for them, and re-layouts: 18.2 us -> 5.66 us
  other arithmetic: 10.7 us -> 0 us
    reduce_scatter x2 -> x0, waiting for transfers between devices: 426 us -> none  [the longest x1 363 us: body(): lax.psum_scatter(jnp.concatenate([grad_k.reshape(count, kv_local * HD), g...]
    all_gather x2 -> x0, blocking collectives: 311 us -> none  [the longest x1 161 us: body(): lax.all_gather(prefix_keys, 'resp', axis=0, tiled=True)]
    pallas_call x0 -> x1, Pallas kernels: none -> 73.1 us  [body(): pl.pallas_call(kernel, name='prefix_gradients', out_shape=(shard, shard,...]
    dot_general x6 -> x0, matrix products: 40.1 us -> none  [the longest x1 13.1 us: body(): jnp.einsum('tkgs,tkgd->skd', dscores, query_heads, preferred_element_type...]
    convert_element_type x1 -> x0, local copies, waits for them, and re-layouts: 12.4 us -> none  [body(): probs_low = probs.astype(jnp.bfloat16)]
  transfers between devices with their start and end apart: 2 -> 0, of which waited for: 2 -> 0; matrix products, arithmetic and copies ran while one was open for 0% -> 0% of each run, Pallas kernels for 0% -> 0%
where the time goes in v1:
time: 80.3 us; the launch traced here: 80.1 us
  Pallas kernels  73.1 us (91%)
  local copies, waits for them, and re-layouts  5.66 us (7%)
  between operations  1.3 us (2%)
    pallas_call x1, Pallas kernels, body(): pl.pallas_call(kernel, name='prefix_gradients', out_shape=(shard, shard,...  73.1 us
    unnamed x11, local copies, waits for them, and re-layouts  5.66 us

profile of v1, /device:TPU:1, one launch (start us, length us, event | category | flops | bytes accessed | tf_op | source)
XLA Modules:
  0.0 80.1 jit_solution(14943817439008677588)
XLA Ops:
  1.3 0.0 copy-start
  1.3 1.2 %copy-done = bf16[256,2048]{1,0:T(8,128)(2,1)S(1)} copy-done((bf16[256,2048]{1,0:T(8,128)(2,1)S(1)}, bf16[256,2048]{1,0:T(8,128)(2,1)}, u32[]{:S(2)}) %copy-start) | copy-done | bytes 1048600
  2.5 0.0 copy-start.1
  2.5 1.2 %copy-done.1 = bf16[256,2048]{1,0:T(8,128)(2,1)S(1)} copy-done((bf16[256,2048]{1,0:T(8,128)(2,1)S(1)}, bf16[256,2048]{1,0:T(8,128)(2,1)}, u32[]{:S(2)}) %copy-start.1) | copy-done | bytes 1048600
  3.7 0.0 copy-start.2
  3.7 0.7 copy-done.2
  4.4 0.0 copy-start.3
  4.4 0.7 copy-done.3
  5.1 73.1 %prefix_gradients.1 = (bf16[16,256]{1,0:T(8,128)(2,1)S(1)}, bf16[16,256]{1,0:T(8,128)(2,1)S(1)}, bf16[16,2048]{1,0:T(8,128)(2,1)S(1)}) custom-call(bf16[256,2048]{1,0:T(8,128)(2,1)S(1)} %copy-done, bf16[256,2048]{1,0:T(8,128)(2,1)S(1)} %copy-done.1, bf16[16,256]{1,0:T(8,128)(2,1)S(1)} %copy-done.2, bf16[16,256]{1,0:T(8,128)(2,1)S(1)} %copy-done.3, ...), custom_call_target="tpu_custom_call" | custom-call | tf_op jit(solution)/shard_map/prefix_gradients/pallas_call | solution.py:256
  78.2 0.6 copy.14
  78.8 0.6 copy.15
  79.4 0.6 copy.16
Async XLA Ops:
  1.3 1.2 %copy-start = (bf16[256,2048]{1,0:T(8,128)(2,1)S(1)}, bf16[256,2048]{1,0:T(8,128)(2,1)}, u32[]{:S(2)}) copy-start(bf16[256,2048]{1,0:T(8,128)(2,1)} %q_hbm.1) | copy-start | bytes 3145732
  2.5 1.2 %copy-start.1 = (bf16[256,2048]{1,0:T(8,128)(2,1)S(1)}, bf16[256,2048]{1,0:T(8,128)(2,1)}, u32[]{:S(2)}) copy-start(bf16[256,2048]{1,0:T(8,128)(2,1)} %g_hbm.1) | copy-start | bytes 3145732
  3.7 0.7 copy-start.2
  4.4 0.7 copy-start.3

commit v2 on v1

v2 whole, which is shorter than its diff:
```python
import functools
import math

import jax
import jax.numpy as jnp
from jax import lax
from jax.experimental import pallas as pl
from jax.experimental.pallas import tpu as pltpu
from jax.sharding import PartitionSpec as P

HD = 128
NY, NX, NZ = 2, 4, 8
NC = 2
N = 8
MESH = pl.DeviceIdType.MESH
SCALE = HD ** (-0.5)
LOG2E = math.log2(math.e)
F32 = jnp.float32
BF16 = jnp.bfloat16


def place():
    r = lax.axis_index("resp")
    return r // (NX * NZ), (r // NZ) % NX, r % NZ, lax.axis_index("head")


def xy_peer(i):
    y, x, z, h = place()
    return ((y + i // NX) % NY * (NX * NZ) + (x + i % NX) % NX * NZ + z, h)


def xy_back(i):
    return i // NX * NX + (-i) % NX


def z_peer(i):
    y, x, z, h = place()
    return (y * (NX * NZ) + x * NZ + (z + i) % NZ, h)


def z_back(i):
    return (-i) % NZ


XY = (xy_peer, xy_back)
Z = (z_peer, z_back)


def head_peer(i):
    y, x, z, h = place()
    return (lax.axis_index("resp"), (h // NC + i // NC) % 2 * NC + (h + i) % NC)


def nt(a, b):
    return lax.dot_general(a, b, (((1,), (1,)), ((), ())), preferred_element_type=F32)


def send(src, dst, ss, rs, to):
    copy = pltpu.make_async_remote_copy(
        src_ref=src, dst_ref=dst, send_sem=ss, recv_sem=rs, device_id=to, device_id_type=MESH
    )
    copy.start()
    return copy


def kernel(
    q_hbm, g_hbm, k_hbm, v_hbm, kw_hbm, vw_hbm, len_ref,
    dk_ref, dv_ref, mine_ref, theirs_ref,
    qs, gs, wts, full, outbox, inbox, partial, inbox2, low, acc,
    e_s, dp_s, m_s, l_s, w_s, d_s, hsend,
    load_sem, own_sem, w_sem, ss, rs, hss, hrs,
):
    heads = qs.shape[0]
    group = heads // 2
    rows = qs.shape[1]

    barrier = pltpu.get_barrier_semaphore()
    for peer, _ in (XY, Z):
        for i in range(1, N):
            pl.semaphore_signal(barrier, inc=1, device_id=peer(i), device_id_type=MESH)
    for i in range(1, 4):
        pl.semaphore_signal(barrier, inc=1, device_id=head_peer(i), device_id_type=MESH)

    own = []
    for j in range(2):
        cols = pl.ds(j * HD, HD)
        own.append(pltpu.make_async_copy(k_hbm.at[:, cols], full.at[j, 0, 0, :, pl.ds(0, HD)], own_sem.at[2 * j]))
        own.append(pltpu.make_async_copy(v_hbm.at[:, cols], full.at[j, 0, 0, :, pl.ds(HD, HD)], own_sem.at[2 * j + 1]))
    for copy in own:
        copy.start()
    loads = []
    for h in range(heads):
        cols = pl.ds(h * HD, HD)
        loads.append(pltpu.make_async_copy(q_hbm.at[:, cols], qs.at[h], load_sem.at[0, h]))
        loads.append(pltpu.make_async_copy(g_hbm.at[:, cols], gs.at[h], load_sem.at[1, h]))
    for copy in loads:
        copy.start()
    weights = []
    for j in (1, 0):
        for i, ref in enumerate((kw_hbm, vw_hbm)):
            weights.append(
                pltpu.make_async_copy(ref.at[:, pl.ds(j * HD, HD)], wts.at[j, :, pl.ds(i * HD, HD)], w_sem.at[j, i])
            )
    for copy in weights:
        copy.start()
    for copy in own:
        copy.wait()
    pl.semaphore_wait(barrier, 2 * (N - 1) + 3)

    sent = []

    def fan(step, j, axes, src_of, dst_of):
        peer, back = axes
        copies = []
        for i in range(1, N):
            copies.append(
                send(src_of(i), dst_of(back(i)), ss.at[step, j, i], rs.at[step, j, back(i)], peer(i))
            )
        sent.extend(copies)
        return copies

    spread_b = fan(0, 1, Z, lambda i: full.at[1, 0, 0], lambda b: full.at[1, 0, b])
    spread_a = fan(0, 0, XY, lambda i: full.at[0, 0, 0], lambda b: full.at[0, b, 0])
    for copy in spread_b:
        copy.wait_recv()
    fan(1, 1, XY, lambda i: full.at[1, 0], lambda b: full.at[1, b])
    for copy in spread_a:
        copy.wait_recv()
    blocks_a = fan(1, 0, Z, lambda i: full.at[0, :, 0], lambda b: full.at[0, :, b])

    for copy in loads:
        copy.wait()
    live = lax.broadcasted_iota(jnp.int32, (rows, HD), 0) < len_ref[0]

    def mask(h, carry):
        grad = gs[h]
        gs[h] = jnp.where(live, grad.astype(F32), 0.0).astype(BF16)
        return carry

    lax.fori_loop(0, heads, mask, 0)

    def softmax_terms(j, c):
        kv = full[j, c].reshape(N * 16, 2 * HD)
        for h in range(group):
            s = nt(kv[:, :HD], qs[j * group + h]) * (SCALE * LOG2E)
            dp = nt(kv[:, HD:], gs[j * group + h])
            m = jnp.max(s, axis=0, keepdims=True)
            e = jnp.exp2(s - m)
            m_s[h, pl.ds(c, 1)] = m
            l_s[h, pl.ds(c, 1)] = jnp.sum(e, axis=0, keepdims=True)
            w_s[h, pl.ds(c, 1)] = jnp.sum(e * dp, axis=0, keepdims=True)
            e_s[h, c] = e
            dp_s[h, c] = dp

    def combine():
        m = m_s[...]
        f = jnp.exp2(m - jnp.max(m, axis=1, keepdims=True))
        total = jnp.sum(f * l_s[...], axis=1, keepdims=True)
        d_s[...] = jnp.sum(f * w_s[...], axis=1, keepdims=True) / total
        m_s[...] = f / total

    def block(j, c):
        back = c // NX * NX + (NX - c % NX) % NX
        return pltpu.make_async_remote_copy(
            src_ref=outbox.at[j, c], dst_ref=inbox.at[j, back],
            send_sem=ss.at[2, j, c], recv_sem=rs.at[2, j, back],
            device_id=xy_peer(c), device_id_type=MESH,
        )

    def gradients(j):
        queries = qs[j * group:(j + 1) * group].reshape(group * rows, HD)
        grads = gs[j * group:(j + 1) * group].reshape(group * rows, HD)

        def one(step, carry):
            c = N - 1 - step
            probs = []
            dscores = []
            for h in range(group):
                p = e_s[h, c] * m_s[h, pl.ds(c, 1)]
                probs.append(p.astype(BF16))
                dscores.append((p * (dp_s[h, c] - d_s[h])).astype(BF16))
            dv = jnp.dot(jnp.concatenate(probs, axis=1), grads, preferred_element_type=F32)
            dk = jnp.dot(jnp.concatenate(dscores, axis=1), queries, preferred_element_type=F32)
            outbox[j, c, :, :, :HD] = (dk * SCALE).astype(BF16).reshape(N, 16, HD)
            outbox[j, c, :, :, HD:] = dv.astype(BF16).reshape(N, 16, HD)

            @pl.when(c > 0)
            def _():
                block(j, c).start()

            return carry

        lax.fori_loop(0, N, one, 0)

    def reduce1(j):
        total = outbox[j, 0].astype(F32)
        for i in range(N - 1, 0, -1):
            block(j, i).wait_recv()
            total += inbox[j, xy_back(i)].astype(F32)
        partial[j] = total.astype(BF16)
        return fan(3, j, Z, lambda i: partial.at[j, i], lambda b: inbox2.at[j, b])

    def reduce2(j, copies):
        total = partial[j, 0].astype(F32)
        for i, copy in enumerate(copies):
            copy.wait_recv()
            total += inbox2[j, z_back(i + 1)].astype(F32)
        total = total.astype(BF16)
        cols = slice(j * HD, (j + 1) * HD)
        low[j] = total
        dk_ref[:, cols] = total[:, :HD]
        dv_ref[:, cols] = total[:, HD:]

    def stream(c, carry):
        @pl.when(c > 0)
        def _():
            pltpu.make_async_remote_copy(
                src_ref=full.at[1, 0], dst_ref=full.at[1, c],
                send_sem=ss.at[1, 1, c], recv_sem=rs.at[1, 1, c],
                device_id=xy_peer(c), device_id_type=MESH,
            ).wait_recv()

        softmax_terms(1, c)
        return carry

    lax.fori_loop(0, N, stream, 0)
    combine()
    gradients(1)
    for copy in blocks_a:
        copy.wait_recv()

    def whole(c, carry):
        softmax_terms(0, c)
        return carry

    lax.fori_loop(0, N, whole, 0)
    combine()
    sums_b = reduce1(1)
    gradients(0)
    sums_a = reduce1(0)
    reduce2(1, sums_b)
    for copy in weights:
        copy.wait()

    width = acc.shape[1] // 4
    step = 512
    low_b = low[1]

    def project(t, carry):
        span = pl.ds(pl.multiple_of(t * step, step), step)
        acc[:, span] = nt(low_b, wts[1, span, :])
        return carry

    lax.fori_loop(0, 4 * width // step, project, 0)
    reduce2(0, sums_a)
    low_a = low[0]
    exchange = []
    for i in (2, 3, 1, 0):
        _, dest = head_peer(i)
        for t in range(width // step):
            span = pl.ds(pl.multiple_of(dest * width + t * step, step), step)
            part = acc[:, span] + nt(low_a, wts[0, span, :])
            if i:
                hsend[i - 1, :, t * step:(t + 1) * step] = part.astype(BF16)
            else:
                mine_ref[:, t * step:(t + 1) * step] = part
        if i:
            exchange.append(
                send(hsend.at[i - 1], theirs_ref.at[i - 1], hss.at[i - 1], hrs.at[i - 1], head_peer(i))
            )
    for copy in exchange:
        copy.wait_recv()
    for copy in sent + exchange:
        copy.wait_send()

    def flushed(c, carry):
        block(0, c).wait_send()
        block(1, c).wait_send()
        return carry

    lax.fori_loop(1, N, flushed, 0)


def finish(dk_ref, dv_ref, mine_ref, theirs_ref, dk_out, dv_out, in_out):
    dk_out[...] = dk_ref[...]
    dv_out[...] = dv_ref[...]
    total = mine_ref[...]
    for i in range(3):
        total += theirs_ref[i].astype(F32)
    in_out[...] = total.astype(BF16)


def body(queries, d_out, prefix_keys, prefix_values, k_weight, v_weight, lengths):
    rows, width = queries.shape
    heads = width // HD
    d = k_weight.shape[0]
    hbm = pl.BlockSpec(memory_space=pltpu.HBM)
    vmem = pl.BlockSpec(memory_space=pltpu.VMEM)
    shard = jax.ShapeDtypeStruct(prefix_keys.shape, BF16)
    parts = pl.pallas_call(
        kernel,
        name="prefix_gradients",
        out_shape=(
            shard,
            shard,
            jax.ShapeDtypeStruct((16, d // 4), F32),
            jax.ShapeDtypeStruct((3, 16, d // 4), BF16),
        ),
        in_specs=[hbm] * 6 + [pl.BlockSpec(memory_space=pltpu.SMEM)],
        out_specs=(vmem,) * 4,
        scratch_shapes=[
            pltpu.VMEM((heads, rows, HD), BF16),
            pltpu.VMEM((heads, rows, HD), BF16),
            pltpu.VMEM((2, d, 2 * HD), BF16),
            pltpu.VMEM((2, N, N, 16, 2 * HD), BF16),
            pltpu.VMEM((2, N, N, 16, 2 * HD), BF16),
            pltpu.VMEM((2, N, N, 16, 2 * HD), BF16),
            pltpu.VMEM((2, N, 16, 2 * HD), BF16),
            pltpu.VMEM((2, N, 16, 2 * HD), BF16),
            pltpu.VMEM((2, 16, 2 * HD), BF16),
            pltpu.VMEM((16, d), F32),
            pltpu.VMEM((heads // 2, N, N * 16, rows), F32),
            pltpu.VMEM((heads // 2, N, N * 16, rows), F32),
            pltpu.VMEM((heads // 2, N, rows), F32),
            pltpu.VMEM((heads // 2, N, rows), F32),
            pltpu.VMEM((heads // 2, N, rows), F32),
            pltpu.VMEM((heads // 2, 1, rows), F32),
            pltpu.VMEM((3, 16, d // 4), BF16),
            pltpu.SemaphoreType.DMA((2, heads)),
            pltpu.SemaphoreType.DMA((4,)),
            pltpu.SemaphoreType.DMA((2, 2)),
            pltpu.SemaphoreType.DMA((4, 2, N)),
            pltpu.SemaphoreType.DMA((4, 2, N)),
            pltpu.SemaphoreType.DMA((3,)),
            pltpu.SemaphoreType.DMA((3,)),
        ],
        compiler_params=pltpu.CompilerParams(
            collective_id=0, has_side_effects=True, vmem_limit_bytes=60 * 1024 * 1024
        ),
    )(queries, d_out, prefix_keys, prefix_values, k_weight, v_weight, lengths)
    return pl.pallas_call(
        finish,
        name="sum_of_heads",
        out_shape=(shard, shard, jax.ShapeDtypeStruct((16, d // 4), BF16)),
        in_specs=[vmem] * 4,
        out_specs=(vmem,) * 3,
    )(*parts)


def solution(mesh):
    placed = (
        P("resp", "head"),
        P("resp", "head"),
        P("resp", "head"),
        P("resp", "head"),
        P(None, "head"),
        P(None, "head"),
        P("resp"),
    )
    return jax.shard_map(
        body,
        mesh=mesh,
        in_specs=placed,
        out_specs=(P("resp", "head"), P("resp", "head"), P("resp", "head")),
        check_vma=False,
    )
```

time: 80.3 us -> 56.1 us (0.70)
  Pallas kernels: 73.1 us -> 54.7 us
  local copies, waits for them, and re-layouts: 5.66 us -> 0 us
    pallas_call x1, Pallas kernels: 73.1 us -> 53 us  [body(): pl.pallas_call(kernel, name='prefix_gradients', out_shape=(shard, shard,...]
    unnamed x11 -> x0, local copies, waits for them, and re-layouts: 5.66 us -> none
    pallas_call x0 -> x1, Pallas kernels: none -> 1.69 us  [body(): pl.pallas_call(finish, name='sum_of_heads', out_shape=(shard, shard, jax....]
where the time goes in v2:
time: 56.1 us; the launch traced here: 56 us
  Pallas kernels  54.7 us (98%)
  between operations  1.29 us (2%)
    pallas_call x1, Pallas kernels, body(): pl.pallas_call(kernel, name='prefix_gradients', out_shape=(shard, shard,...  53 us
    pallas_call x1, Pallas kernels, body(): pl.pallas_call(finish, name='sum_of_heads', out_shape=(shard, shard, jax....  1.69 us

profile of v2, /device:TPU:1, one launch (start us, length us, event | category | flops | bytes accessed | tf_op | source)
XLA Modules:
  0.0 56.0 jit_solution(5599900644218805382)
XLA Ops:
  1.3 53.0 %prefix_gradients.1 = (bf16[16,256]{1,0:T(8,128)(2,1)}, bf16[16,256]{1,0:T(8,128)(2,1)}, f32[16,2048]{1,0:T(8,128)}, bf16[3,16,2048]{2,1,0:T(8,128)(2,1)}) custom-call(bf16[256,2048]{1,0:T(8,128)(2,1)} %q_hbm.1, bf16[256,2048]{1,0:T(8,128)(2,1)} %g_hbm.1, bf16[16,256]{1,0:T(8,128)(2,1)} %k_hbm.1, bf16[16,256]{1,0:T(8,128)(2,1)} %v_hbm.1, ...), custom_call_target="tpu_custom_call" | custom-call | tf_op jit(solution)/shard_map/prefix_gradients/pallas_call | solution.py:300
  54.3 1.7 %sum_of_heads.1 = (bf16[16,256]{1,0:T(8,128)(2,1)}, bf16[16,256]{1,0:T(8,128)(2,1)}, bf16[16,2048]{1,0:T(8,128)(2,1)}) custom-call(bf16[16,256]{1,0:T(8,128)(2,1)} %get-tuple-element.7.dk_ref, bf16[16,256]{1,0:T(8,128)(2,1)} %get-tuple-element.8.dv_ref, f32[16,2048]{1,0:T(8,128)} %get-tuple-element.9.mine_ref, bf16[3,16,2048]{2,1,0:T(8,128)(2,1)} %get-tuple-element.10.theirs_ref), custom_call_target="tpu_custom_call" | custom-call | tf_op jit(solution)/shard_map/sum_of_heads/pallas_call | solution.py:341

commit v3 on v2

--- a/solution.py
+++ b/solution.py
@@ -11,6 +11,7 @@
 HD = 128
 NY, NX, NZ = 2, 4, 8
 NC = 2
+CHUNK = 128
 N = 8
 MESH = pl.DeviceIdType.MESH
 SCALE = HD ** (-0.5)
@@ -64,15 +65,14 @@
 
 
 def kernel(
-    q_hbm, g_hbm, k_hbm, v_hbm, kw_hbm, vw_hbm, len_ref,
+    q_hbm, g_hbm, k_hbm, v_hbm, kw_hbm, vw_hbm, len_hbm,
     dk_ref, dv_ref, mine_ref, theirs_ref,
     qs, gs, wts, full, outbox, inbox, partial, inbox2, low, acc,
-    e_s, dp_s, m_s, l_s, w_s, d_s, hsend,
+    e_s, dp_s, m_s, l_s, w_s, d_s, hsend, len_ref,
     load_sem, own_sem, w_sem, ss, rs, hss, hrs,
 ):
-    heads = qs.shape[0]
-    group = heads // 2
-    rows = qs.shape[1]
+    rows, columns = qs.shape
+    group = columns // HD // 2
 
     barrier = pltpu.get_barrier_semaphore()
     for peer, _ in (XY, Z):
@@ -88,11 +88,11 @@
         own.append(pltpu.make_async_copy(v_hbm.at[:, cols], full.at[j, 0, 0, :, pl.ds(HD, HD)], own_sem.at[2 * j + 1]))
     for copy in own:
         copy.start()
-    loads = []
-    for h in range(heads):
-        cols = pl.ds(h * HD, HD)
-        loads.append(pltpu.make_async_copy(q_hbm.at[:, cols], qs.at[h], load_sem.at[0, h]))
-        loads.append(pltpu.make_async_copy(g_hbm.at[:, cols], gs.at[h], load_sem.at[1, h]))
+    loads = [
+        pltpu.make_async_copy(q_hbm, qs, load_sem.at[0]),
+        pltpu.make_async_copy(g_hbm, gs, load_sem.at[1]),
+        pltpu.make_async_copy(len_hbm, len_ref, load_sem.at[2]),
+    ]
     for copy in loads:
         copy.start()
     weights = []
@@ -130,27 +130,40 @@
 
     for copy in loads:
         copy.wait()
-    live = lax.broadcasted_iota(jnp.int32, (rows, HD), 0) < len_ref[0]
-
-    def mask(h, carry):
-        grad = gs[h]
-        gs[h] = jnp.where(live, grad.astype(F32), 0.0).astype(BF16)
+    length = len_ref[0]
+    slab = 16
+
+    def mask(i, carry):
+        base = pl.multiple_of(i * slab, slab)
+        live = lax.broadcasted_iota(jnp.int32, (slab, columns), 0) + base < length
+        grad = gs[pl.ds(base, slab), :]
+        gs[pl.ds(base, slab), :] = jnp.where(live, grad.astype(F32), 0.0).astype(BF16)
         return carry
 
-    lax.fori_loop(0, heads, mask, 0)
-
-    def softmax_terms(j, c):
-        kv = full[j, c].reshape(N * 16, 2 * HD)
+    lax.fori_loop(0, rows // slab, mask, 0)
+
+    def head(ref, j, h):
+        return ref[:, (j * group + h) * HD:(j * group + h + 1) * HD]
+
+    def stacked(ref, j):
+        return jnp.concatenate([head(ref, j, h) for h in range(group)], axis=0)
+
+    def softmax_terms(j, first, count):
+        kv = full[j, pl.ds(first, count)].reshape(count * CHUNK, 2 * HD)
         for h in range(group):
-            s = nt(kv[:, :HD], qs[j * group + h]) * (SCALE * LOG2E)
-            dp = nt(kv[:, HD:], gs[j * group + h])
-            m = jnp.max(s, axis=0, keepdims=True)
-            e = jnp.exp2(s - m)
-            m_s[h, pl.ds(c, 1)] = m
-            l_s[h, pl.ds(c, 1)] = jnp.sum(e, axis=0, keepdims=True)
-            w_s[h, pl.ds(c, 1)] = jnp.sum(e * dp, axis=0, keepdims=True)
-            e_s[h, c] = e
-            dp_s[h, c] = dp
+            scores = nt(kv[:, :HD], head(qs, j, h)) * (SCALE * LOG2E)
+            dprobs = nt(kv[:, HD:], head(gs, j, h))
+            for i in range(count):
+                c = first + i
+                s = scores[i * CHUNK:(i + 1) * CHUNK]
+                dp = dprobs[i * CHUNK:(i + 1) * CHUNK]
+                m = jnp.max(s, axis=0, keepdims=True)
+                e = jnp.exp2(s - m)
+                m_s[h, pl.ds(c, 1)] = m
+                l_s[h, pl.ds(c, 1)] = jnp.sum(e, axis=0, keepdims=True)
+                w_s[h, pl.ds(c, 1)] = jnp.sum(e * dp, axis=0, keepdims=True)
+                e_s[h, c] = e
+                dp_s[h, c] = dp
 
     def combine():
         m = m_s[...]
@@ -167,30 +180,36 @@
             device_id=xy_peer(c), device_id_type=MESH,
         )
 
-    def gradients(j):
-        queries = qs[j * group:(j + 1) * group].reshape(group * rows, HD)
-        grads = gs[j * group:(j + 1) * group].reshape(group * rows, HD)
-
+    def gradients(j, count):
         def one(step, carry):
-            c = N - 1 - step
+            first = N - count * (step + 1)
             probs = []
             dscores = []
             for h in range(group):
-                p = e_s[h, c] * m_s[h, pl.ds(c, 1)]
-                probs.append(p.astype(BF16))
-                dscores.append((p * (dp_s[h, c] - d_s[h])).astype(BF16))
-            dv = jnp.dot(jnp.concatenate(probs, axis=1), grads, preferred_element_type=F32)
-            dk = jnp.dot(jnp.concatenate(dscores, axis=1), queries, preferred_element_type=F32)
-            outbox[j, c, :, :, :HD] = (dk * SCALE).astype(BF16).reshape(N, 16, HD)
-            outbox[j, c, :, :, HD:] = dv.astype(BF16).reshape(N, 16, HD)
-
-            @pl.when(c > 0)
+                for i in range(count):
+                    p = e_s[h, first + i] * m_s[h, pl.ds(first + i, 1)]
+                    probs.append(p.astype(BF16))
+                    dscores.append((p * (dp_s[h, first + i] - d_s[h])).astype(BF16))
+
+            def whole(parts):
+                columns = [jnp.concatenate(parts[h * count:(h + 1) * count], axis=0) for h in range(group)]
+                return jnp.concatenate(columns, axis=1)
+
+            dv = jnp.dot(whole(probs), stacked(gs, j), preferred_element_type=F32)
+            dk = jnp.dot(whole(dscores), stacked(qs, j), preferred_element_type=F32)
+            span = pl.ds(first, count)
+            outbox[j, span, :, :, :HD] = (dk * SCALE).astype(BF16).reshape(count, N, 16, HD)
+            outbox[j, span, :, :, HD:] = dv.astype(BF16).reshape(count, N, 16, HD)
+            for i in range(count - 1, 0, -1):
+                block(j, first + i).start()
+
+            @pl.when(first > 0)
             def _():
-                block(j, c).start()
+                block(j, first).start()
 
             return carry
 
-        lax.fori_loop(0, N, one, 0)
+        lax.fori_loop(0, N // count, one, 0)
 
     def reduce1(j):
         total = outbox[j, 0].astype(F32)
@@ -220,28 +239,39 @@
                 device_id=xy_peer(c), device_id_type=MESH,
             ).wait_recv()
 
-        softmax_terms(1, c)
+        softmax_terms(1, c, 1)
         return carry
 
     lax.fori_loop(0, N, stream, 0)
     combine()
-    gradients(1)
+    gradients(1, 4)
     for copy in blocks_a:
         copy.wait_recv()
 
-    def whole(c, carry):
-        softmax_terms(0, c)
+    def rest(i, carry):
+        softmax_terms(0, i * 4, 4)
         return carry
 
-    lax.fori_loop(0, N, whole, 0)
+    lax.fori_loop(0, N // 4, rest, 0)
     combine()
+    gradients(0, 4)
     sums_b = reduce1(1)
-    gradients(0)
     sums_a = reduce1(0)
     reduce2(1, sums_b)
     for copy in weights:
         copy.wait()
 
+    def flush():
+        for copy in sent[:-2 * (N - 1)]:
+            copy.wait_send()
+
+        def flushed(c, carry):
+            block(1, c).wait_send()
+            block(0, c).wait_send()
+            return carry
+
+        lax.fori_loop(1, N, flushed, 0)
+
     width = acc.shape[1] // 4
     step = 512
     low_b = low[1]
@@ -252,6 +282,7 @@
         return carry
 
     lax.fori_loop(0, 4 * width // step, project, 0)
+    flush()
     reduce2(0, sums_a)
     low_a = low[0]
     exchange = []
@@ -270,15 +301,8 @@
             )
     for copy in exchange:
         copy.wait_recv()
-    for copy in sent + exchange:
+    for copy in sent[-2 * (N - 1):] + exchange:
         copy.wait_send()
-
-    def flushed(c, carry):
-        block(0, c).wait_send()
-        block(1, c).wait_send()
-        return carry
-
-    lax.fori_loop(1, N, flushed, 0)
 
 
 def finish(dk_ref, dv_ref, mine_ref, theirs_ref, dk_out, dv_out, in_out):
@@ -306,11 +330,11 @@
             jax.ShapeDtypeStruct((16, d // 4), F32),
             jax.ShapeDtypeStruct((3, 16, d // 4), BF16),
         ),
-        in_specs=[hbm] * 6 + [pl.BlockSpec(memory_space=pltpu.SMEM)],
+        in_specs=[hbm] * 7,
         out_specs=(vmem,) * 4,
         scratch_shapes=[
-            pltpu.VMEM((heads, rows, HD), BF16),
-            pltpu.VMEM((heads, rows, HD), BF16),
+            pltpu.VMEM((rows, width), BF16),
+            pltpu.VMEM((rows, width), BF16),
             pltpu.VMEM((2, d, 2 * HD), BF16),
             pltpu.VMEM((2, N, N, 16, 2 * HD), BF16),
             pltpu.VMEM((2, N, N, 16, 2 * HD), BF16),
@@ -326,7 +350,8 @@
             pltpu.VMEM((heads // 2, N, rows), F32),
             pltpu.VMEM((heads // 2, 1, rows), F32),
             pltpu.VMEM((3, 16, d // 4), BF16),
-            pltpu.SemaphoreType.DMA((2, heads)),
+            pltpu.SMEM((1,), jnp.int32),
+            pltpu.SemaphoreType.DMA((3,)),
             pltpu.SemaphoreType.DMA((4,)),
             pltpu.SemaphoreType.DMA((2, 2)),
             pltpu.SemaphoreType.DMA((4, 2, N)),

time: 56.1 us -> 53.9 us (0.961)
  Pallas kernels: 54.7 us -> 52.5 us
    pallas_call x1, Pallas kernels: 53 us -> 50.8 us  [body(): pl.pallas_call(kernel, name='prefix_gradients', out_shape=(shard, shard,...]
where the time goes in v3:
time: 53.9 us; the launch traced here: 53.8 us
  Pallas kernels  52.5 us (97%)
  between operations  1.29 us (2%)
    pallas_call x1, Pallas kernels, body(): pl.pallas_call(kernel, name='prefix_gradients', out_shape=(shard, shard,...  50.8 us
    pallas_call x1, Pallas kernels, body(): pl.pallas_call(finish, name='sum_of_heads', out_shape=(shard, shard, jax....  1.69 us

profile of v3, /device:TPU:1, one launch (start us, length us, event | category | flops | bytes accessed | tf_op | source)
XLA Modules:
  0.0 53.8 jit_solution(15189229094880151599)
XLA Ops:
  1.3 50.8 %prefix_gradients.1 = (bf16[16,256]{1,0:T(8,128)(2,1)}, bf16[16,256]{1,0:T(8,128)(2,1)}, f32[16,2048]{1,0:T(8,128)}, bf16[3,16,2048]{2,1,0:T(8,128)(2,1)}) custom-call(bf16[256,2048]{1,0:T(8,128)(2,1)} %q_hbm.1, bf16[256,2048]{1,0:T(8,128)(2,1)} %g_hbm.1, bf16[16,256]{1,0:T(8,128)(2,1)} %k_hbm.1, bf16[16,256]{1,0:T(8,128)(2,1)} %v_hbm.1, ...), custom_call_target="tpu_custom_call" | custom-call | tf_op jit(solution)/shard_map/prefix_gradients/pallas_call | solution.py:324
  52.1 1.7 %sum_of_heads.1 = (bf16[16,256]{1,0:T(8,128)(2,1)}, bf16[16,256]{1,0:T(8,128)(2,1)}, bf16[16,2048]{1,0:T(8,128)(2,1)}) custom-call(bf16[16,256]{1,0:T(8,128)(2,1)} %get-tuple-element.7.dk_ref, bf16[16,256]{1,0:T(8,128)(2,1)} %get-tuple-element.8.dv_ref, f32[16,2048]{1,0:T(8,128)} %get-tuple-element.9.mine_ref, bf16[3,16,2048]{2,1,0:T(8,128)(2,1)} %get-tuple-element.10.theirs_ref), custom_call_target="tpu_custom_call" | custom-call | tf_op jit(solution)/shard_map/sum_of_heads/pallas_call | solution.py:366

commit v4 on v3

--- a/solution.py
+++ b/solution.py
@@ -47,6 +47,9 @@
 Z = (z_peer, z_back)
 
 
+FAR_FIRST = ((6, 5, 7, 2, 4, 1, 3), (4, 3, 5, 2, 6, 1, 7))
+
+
 def head_peer(i):
     y, x, z, h = place()
     return (lax.axis_index("resp"), (h // NC + i // NC) % 2 * NC + (h + i) % NC)
@@ -75,9 +78,10 @@
     group = columns // HD // 2
 
     barrier = pltpu.get_barrier_semaphore()
-    for peer, _ in (XY, Z):
-        for i in range(1, N):
-            pl.semaphore_signal(barrier, inc=1, device_id=peer(i), device_id_type=MESH)
+    for i in (4, 3, 5, 2, 6, 1, 7):
+        pl.semaphore_signal(barrier, inc=1, device_id=z_peer(i), device_id_type=MESH)
+    for i in (6, 5, 7, 2, 4, 1, 3):
+        pl.semaphore_signal(barrier, inc=1, device_id=xy_peer(i), device_id_type=MESH)
     for i in range(1, 4):
         pl.semaphore_signal(barrier, inc=1, device_id=head_peer(i), device_id_type=MESH)
 
@@ -112,7 +116,7 @@
     def fan(step, j, axes, src_of, dst_of):
         peer, back = axes
         copies = []
-        for i in range(1, N):
+        for i in FAR_FIRST[axes is Z]:
             copies.append(
                 send(src_of(i), dst_of(back(i)), ss.at[step, j, i], rs.at[step, j, back(i)], peer(i))
             )
@@ -221,9 +225,9 @@
 
     def reduce2(j, copies):
         total = partial[j, 0].astype(F32)
-        for i, copy in enumerate(copies):
+        for i, copy in zip(FAR_FIRST[1], copies):
             copy.wait_recv()
-            total += inbox2[j, z_back(i + 1)].astype(F32)
+            total += inbox2[j, z_back(i)].astype(F32)
         total = total.astype(BF16)
         cols = slice(j * HD, (j + 1) * HD)
         low[j] = total
@@ -244,7 +248,7 @@
 
     lax.fori_loop(0, N, stream, 0)
     combine()
-    gradients(1, 4)
+    gradients(1, 2)
     for copy in blocks_a:
         copy.wait_recv()
 
@@ -254,7 +258,7 @@
 
     lax.fori_loop(0, N // 4, rest, 0)
     combine()
-    gradients(0, 4)
+    gradients(0, 2)
     sums_b = reduce1(1)
     sums_a = reduce1(0)
     reduce2(1, sums_b)

time: 53.9 us -> 54.3 us (level)
  no operation moved by 1% of the time
where the time goes in v4:
time: 54.3 us; the launch traced here: 54.2 us
  Pallas kernels  53 us (98%)
  between operations  1.29 us (2%)
    pallas_call x1, Pallas kernels, body(): pl.pallas_call(kernel, name='prefix_gradients', out_shape=(shard, shard,...  51.3 us
    pallas_call x1, Pallas kernels, body(): pl.pallas_call(finish, name='sum_of_heads', out_shape=(shard, shard, jax....  1.69 us

profile of v4, /device:TPU:1, one launch (start us, length us, event | category | flops | bytes accessed | tf_op | source)
XLA Modules:
  0.0 54.2 jit_solution(3149020565110513211)
XLA Ops:
  1.3 51.3 %prefix_gradients.1 = (bf16[16,256]{1,0:T(8,128)(2,1)}, bf16[16,256]{1,0:T(8,128)(2,1)}, f32[16,2048]{1,0:T(8,128)}, bf16[3,16,2048]{2,1,0:T(8,128)(2,1)}) custom-call(bf16[256,2048]{1,0:T(8,128)(2,1)} %q_hbm.1, bf16[256,2048]{1,0:T(8,128)(2,1)} %g_hbm.1, bf16[16,256]{1,0:T(8,128)(2,1)} %k_hbm.1, bf16[16,256]{1,0:T(8,128)(2,1)} %v_hbm.1, ...), custom_call_target="tpu_custom_call" | custom-call | tf_op jit(solution)/shard_map/prefix_gradients/pallas_call | solution.py:328
  52.5 1.7 %sum_of_heads.1 = (bf16[16,256]{1,0:T(8,128)(2,1)}, bf16[16,256]{1,0:T(8,128)(2,1)}, bf16[16,2048]{1,0:T(8,128)(2,1)}) custom-call(bf16[16,256]{1,0:T(8,128)(2,1)} %get-tuple-element.7.dk_ref, bf16[16,256]{1,0:T(8,128)(2,1)} %get-tuple-element.8.dv_ref, f32[16,2048]{1,0:T(8,128)} %get-tuple-element.9.mine_ref, bf16[3,16,2048]{2,1,0:T(8,128)(2,1)} %get-tuple-element.10.theirs_ref), custom_call_target="tpu_custom_call" | custom-call | tf_op jit(solution)/shard_map/sum_of_heads/pallas_call | solution.py:370

commit v5 on v3

--- a/solution.py
+++ b/solution.py
@@ -121,26 +121,26 @@
 
     spread_b = fan(0, 1, Z, lambda i: full.at[1, 0, 0], lambda b: full.at[1, 0, b])
     spread_a = fan(0, 0, XY, lambda i: full.at[0, 0, 0], lambda b: full.at[0, b, 0])
+    for copy in loads:
+        copy.wait()
+    length = len_ref[0]
+    slab = 16
+
+    def mask(i, carry):
+        base = pl.multiple_of(i * slab, slab)
+        live = lax.broadcasted_iota(jnp.int32, (slab, columns), 0) + base < length
+        grad = gs[pl.ds(base, slab), :]
+        gs[pl.ds(base, slab), :] = jnp.where(live, grad.astype(F32), 0.0).astype(BF16)
+        return carry
+
+    lax.fori_loop(0, rows // slab, mask, 0)
+
     for copy in spread_b:
         copy.wait_recv()
     fan(1, 1, XY, lambda i: full.at[1, 0], lambda b: full.at[1, b])
     for copy in spread_a:
         copy.wait_recv()
     blocks_a = fan(1, 0, Z, lambda i: full.at[0, :, 0], lambda b: full.at[0, :, b])
-
-    for copy in loads:
-        copy.wait()
-    length = len_ref[0]
-    slab = 16
-
-    def mask(i, carry):
-        base = pl.multiple_of(i * slab, slab)
-        live = lax.broadcasted_iota(jnp.int32, (slab, columns), 0) + base < length
-        grad = gs[pl.ds(base, slab), :]
-        gs[pl.ds(base, slab), :] = jnp.where(live, grad.astype(F32), 0.0).astype(BF16)
-        return carry
-
-    lax.fori_loop(0, rows // slab, mask, 0)
 
     def head(ref, j, h):
         return ref[:, (j * group + h) * HD:(j * group + h + 1) * HD]

time: 53.9 us -> 53.9 us (level)
  no operation moved by 1% of the time
where the time goes in v5:
time: 53.9 us; the launch traced here: 53.8 us
  Pallas kernels  52.5 us (97%)
  between operations  1.29 us (2%)
    pallas_call x1, Pallas kernels, body(): pl.pallas_call(kernel, name='prefix_gradients', out_shape=(shard, shard,...  50.8 us
    pallas_call x1, Pallas kernels, body(): pl.pallas_call(finish, name='sum_of_heads', out_shape=(shard, shard, jax....  1.69 us

profile of v5, /device:TPU:1, one launch (start us, length us, event | category | flops | bytes accessed | tf_op | source)
XLA Modules:
  0.0 53.8 jit_solution(18322945567421139367)
XLA Ops:
  1.3 50.8 %prefix_gradients.1 = (bf16[16,256]{1,0:T(8,128)(2,1)}, bf16[16,256]{1,0:T(8,128)(2,1)}, f32[16,2048]{1,0:T(8,128)}, bf16[3,16,2048]{2,1,0:T(8,128)(2,1)}) custom-call(bf16[256,2048]{1,0:T(8,128)(2,1)} %q_hbm.1, bf16[256,2048]{1,0:T(8,128)(2,1)} %g_hbm.1, bf16[16,256]{1,0:T(8,128)(2,1)} %k_hbm.1, bf16[16,256]{1,0:T(8,128)(2,1)} %v_hbm.1, ...), custom_call_target="tpu_custom_call" | custom-call | tf_op jit(solution)/shard_map/prefix_gradients/pallas_call | solution.py:324
  52.1 1.7 %sum_of_heads.1 = (bf16[16,256]{1,0:T(8,128)(2,1)}, bf16[16,256]{1,0:T(8,128)(2,1)}, bf16[16,2048]{1,0:T(8,128)(2,1)}) custom-call(bf16[16,256]{1,0:T(8,128)(2,1)} %get-tuple-element.7.dk_ref, bf16[16,256]{1,0:T(8,128)(2,1)} %get-tuple-element.8.dv_ref, f32[16,2048]{1,0:T(8,128)} %get-tuple-element.9.mine_ref, bf16[3,16,2048]{2,1,0:T(8,128)(2,1)} %get-tuple-element.10.theirs_ref), custom_call_target="tpu_custom_call" | custom-call | tf_op jit(solution)/shard_map/sum_of_heads/pallas_call | solution.py:366
